TPU v7x, 32 devices: a whole 2x2x4 slice. The times are simulated.
32 devices in a mesh: replica: 2 (over x), pool: 16 (over z, y, core).
Axes of the slice: x: 2, y: 2, z: 4, core: 2. Of those that a mesh axis runs over, the one named last changes fastest.
Arguments:
- stretch_queries: bfloat16 [4096, 8192], P(('replica', 'pool')), parts along dimension 0, may hold values from -7 to 7
- decode_queries: bfloat16 [128, 8192], P(('replica', 'pool')), parts along dimension 0, may hold values from -7 to 7
- stretch_entries: bfloat16 [2, 4096, 1024], P(None, ('replica', 'pool')), parts along dimension 1, may hold values from -7 to 7
- decode_entries: bfloat16 [2, 128, 1024], P(None, ('replica', 'pool')), parts along dimension 1, may hold values from -7 to 7
- pool_pages: bfloat16 [2048, 2, 16, 1024], P(('replica', 'pool')), parts along dimension 0, may hold values from -7 to 7
- page_owner: int32 [3072, 1], P(('replica', 'pool')), parts along dimension 0, may hold values from 0 to 15; in each aligned block of 96 rows (0 to 95, 96 to 191, ...) at most 8 rows name the same one
- page_slot: int32 [3072], P(('replica', 'pool')), parts along dimension 0, may hold values from 0 to 63
- prefix_length: int32 [32], P(('replica', 'pool')), parts along dimension 0, may hold values from 0 to 768, as said below
- context_length: int32 [128], P(('replica', 'pool')), parts along dimension 0, may hold values from 1 to 192, as said below
Outputs:
- stretch_output: bfloat16 [4096, 8192], P(('replica', 'pool')), parts along dimension 0
- decode_output: bfloat16 [128, 8192], P(('replica', 'pool')), parts along dimension 0
There are 2 independent parts, one for each index of `replica`. A program takes and returns all parts, laid end to end along the dimension named above; each array names one. Nothing has to cross between parts.
Inputs may be any that keep to these rules, and one draw needn't show every extreme that they name: `page_owner`: in the 96 rows of one device no owner appears more than 8 times; in some devices' rows one owner appears exactly 8 times. `prefix_length`: some batch shard has the full 48 * 16 prefix positions. `context_length`: some decode row has the full 12 * 16 positions.
All inputs are finite; a program needn't handle non-finite values.
Results may differ from a plain program's by a relative error of at most 0.0046.
Values may be sent and summed in bfloat16 or wider, within the bound.
A program may use at most 192 MiB of HBM per device.

v0:
```python
import jax
import jax.numpy as jnp
from jax import lax
from jax.sharding import PartitionSpec as P

HEADS = 64
HEAD_DIM = 128
PRE_PAGES = 48
DEC_PAGES = 12


def attend(queries, parts):
    row_count = queries.shape[0]
    key_heads = parts[0][0].shape[-1] // HEAD_DIM
    group_size = HEADS // key_heads
    factor = 1.0 / HEAD_DIM**0.5
    results = []
    for head_index in range(key_heads):
        lower = head_index * group_size * HEAD_DIM
        upper = lower + group_size * HEAD_DIM
        head_queries = queries[:, lower:upper].reshape(row_count, group_size, HEAD_DIM)
        scores = []
        for keys, values, usable in parts:
            key_part = keys[..., head_index * HEAD_DIM : (head_index + 1) * HEAD_DIM]
            if key_part.ndim == 2:
                score = jnp.einsum(
                    "rgd,ld->grl", head_queries, key_part, preferred_element_type=jnp.float32
                )
            else:
                score = jnp.einsum(
                    "rgd,rld->grl", head_queries, key_part, preferred_element_type=jnp.float32
                )
            scores.append(jnp.where(usable[None], score * factor, -jnp.inf))
        joined = jnp.concatenate(scores, axis=2)
        highest = jnp.max(joined, axis=2, keepdims=True)
        terms = jnp.exp(joined - highest)
        totals = jnp.sum(terms, axis=2)
        rounded = terms.astype(jnp.bfloat16)
        summed = jnp.zeros((row_count, group_size, HEAD_DIM), jnp.float32)
        offset = 0
        for keys, values, usable in parts:
            length = keys.shape[-2]
            weight_part = rounded[:, :, offset : offset + length]
            value_part = values[..., head_index * HEAD_DIM : (head_index + 1) * HEAD_DIM]
            if value_part.ndim == 2:
                summed = summed + jnp.einsum(
                    "grl,ld->rgd", weight_part, value_part, preferred_element_type=jnp.float32
                )
            else:
                summed = jnp.einsum(
                    "grl,rld->rgd", weight_part, value_part, preferred_element_type=jnp.float32
                )
            offset = offset + length
        results.append(
            (summed / jnp.transpose(totals)[:, :, None]).reshape(row_count, group_size * HEAD_DIM)
        )
    return jnp.concatenate(results, axis=1).astype(jnp.bfloat16)


def on_device(
    stretch_queries,
    decode_queries,
    stretch_entries,
    decode_entries,
    pool_pages,
    page_owner,
    page_slot,
    prefix_length,
    context_length,
):
    pool_size = lax.axis_size("pool")
    page_count = page_slot.shape[0]
    capacity = max(2, 4 * page_count // (3 * pool_size))
    slot_total = pool_size * capacity
    page_tokens = pool_pages.shape[2]
    key_width = pool_pages.shape[3]
    owners = page_owner[:, 0]
    member = (owners[:, None] == jnp.arange(pool_size, dtype=jnp.int32)[None, :]).astype(jnp.int32)
    ranks = jnp.sum(jnp.cumsum(member, axis=0) * member, axis=1) - 1
    target = owners * capacity + ranks
    placed = target[:, None] == jnp.arange(slot_total, dtype=jnp.int32)[None, :]
    requests = jnp.sum(jnp.where(placed, page_slot[:, None], 0), axis=0).reshape(
        pool_size, capacity
    )
    incoming = lax.all_to_all(requests, "pool", split_axis=0, concat_axis=0, tiled=True)
    served = jnp.take(pool_pages, incoming.reshape(-1), axis=0).reshape(
        (pool_size, capacity) + pool_pages.shape[1:]
    )
    received = lax.all_to_all(served, "pool", split_axis=0, concat_axis=0, tiled=True)
    received = received.reshape((slot_total,) + pool_pages.shape[1:])
    stretch_count = stretch_queries.shape[0]
    decode_count = decode_queries.shape[0]
    causal = jnp.arange(stretch_count)[:, None] >= jnp.arange(stretch_count)[None, :]
    own_usable = jnp.ones((decode_count, 1), dtype=jnp.bool_)
    used = jnp.any(placed, axis=0)
    page_of = jnp.sum(
        jnp.where(placed, jnp.arange(page_count, dtype=jnp.int32)[:, None], 0), axis=0
    )
    within = jnp.arange(page_tokens, dtype=jnp.int32)[None, :]
    prefix_usable = (
        used[:, None]
        & (page_of[:, None] < PRE_PAGES)
        & (page_of[:, None] * page_tokens + within < prefix_length[0])
    ).reshape(1, slot_total * page_tokens)
    cache_index = page_of - PRE_PAGES
    row_owner = cache_index // DEC_PAGES
    cache_position = (cache_index % DEC_PAGES)[:, None] * page_tokens + within
    slot_ok = (used & (cache_index >= 0))[None, :, None]
    row_match = row_owner[None, :, None] == jnp.arange(decode_count, dtype=jnp.int32)[:, None, None]
    length_ok = cache_position[None] < context_length[:, None, None]
    cache_usable = (slot_ok & row_match & length_ok).reshape(decode_count, slot_total * page_tokens)
    prefix_keys = received[:, 0].reshape(slot_total * page_tokens, key_width)
    prefix_values = received[:, 1].reshape(slot_total * page_tokens, key_width)
    stretch_output = attend(
        stretch_queries,
        [
            (stretch_entries[0], stretch_entries[1], causal),
            (prefix_keys, prefix_values, prefix_usable),
        ],
    )
    decode_output = attend(
        decode_queries,
        [
            (decode_entries[0][:, None, :], decode_entries[1][:, None, :], own_usable),
            (prefix_keys, prefix_values, cache_usable),
        ],
    )
    return (stretch_output, decode_output)


def solution(mesh):
    placed = (
        P(("replica", "pool"), None),
        P(("replica", "pool"), None),
        P(None, ("replica", "pool"), None),
        P(None, ("replica", "pool"), None),
        P(("replica", "pool"), None, None, None),
        P(("replica", "pool"), None),
        P(("replica", "pool")),
        P(("replica", "pool")),
        P(("replica", "pool")),
    )
    return jax.shard_map(
        on_device,
        mesh=mesh,
        in_specs=placed,
        out_specs=(P(("replica", "pool"), None), P(("replica", "pool"), None)),
        check_vma=False,
    )
```

profile of v0, /device:TPU:9, one launch (start us, length us, event | category | flops | bytes accessed | tf_op | source)
XLA Modules:
  0.0 389.5 jit_solution(5156140764221701054)
XLA Ops:
  3.9 11.1 %all_to_all.14 = s32[16,1,8]{2,1,0:T(1,128)S(1)} all-to-all(s32[16,1,8]{2,1,0:T(1,128)S(1)} %bitcast.807), channel_id=1, replica_groups=mesh['replica'=2,'pool'=16] {'pool'}, dimensions={0} | all-to-all | bytes 1024 | tf_op jit(solution)/shard_map/all_to_all | solution.py:85
  16.4 8.6 %gather_fusion = bf16[128,2,16,1024]{3,2,1,0:T(8,128)(2,1)} fusion(bf16[64,2,16,1024]{3,2,1,0:T(8,128)(2,1)} %param.13, s32[1024]{0:T(1024)S(1)} %pad_clamp_fusion), kind=kCustom, calls=%fused_computation | custom fusion | bytes 16777728 | tf_op jit(solution)/shard_map/jit(_take)/gather | solution.py:86
  25.0 7.4 %broadcast_select_fusion = bf16[16,8,2,16,1024]{4,3,2,1,0:T(8,128)(2,1)} fusion(bf16[16,8,2,16,1024]{4,3,2,1,0:T(8,128)(2,1)} %bitcast.733, pred[16,8]{1,0:T(8,128)(4,1)S(1)} %copy.323), kind=kLoop, calls=%fused_computation.25 | loop fusion | flops 4194304 | bytes 16777344 | tf_op jit(solution)/shard_map/jit(_take)/select_n | solution.py:86
  32.5 8.5 %copy.324 = bf16[16,8,2,16,1024]{4,3,1,2,0:T(8,128)(2,1)} copy(bf16[16,8,2,16,1024]{4,3,2,1,0:T(8,128)(2,1)} %broadcast_select_fusion) | data formatting | bytes 16777216 | tf_op jit(solution)/shard_map/jit(_take)/select_n | solution.py:86
  41.0 6.6 %all-to-all-start.1 = ((bf16[16,8,2,16,1024]{4,3,1,2,0:T(8,128)(2,1)}), bf16[16,8,2,16,1024]{4,3,1,2,0:T(8,128)(2,1)}, u32[]{:S(2)}, u32[]{:S(2)}) async-start(bf16[16,8,2,16,1024]{4,3,1,2,0:T(8,128)(2,1)} %copy.324), calls=%async_computation.1 | async-start | bytes 16777216 | tf_op jit(solution)/shard_map/all_to_all | solution.py:89
  57.5 1.8 fusion.257
  64.0 2.4 fusion.272
  66.3 2.4 fusion.270
  68.7 2.4 fusion.268
  71.1 1.6 fusion.266
  72.7 1.6 fusion.264
  74.3 1.6 fusion.262
  76.4 151.3 %all-to-all-done.1 = bf16[16,8,2,16,1024]{4,3,1,2,0:T(8,128)(2,1)} async-done(((bf16[16,8,2,16,1024]{4,3,1,2,0:T(8,128)(2,1)}), bf16[16,8,2,16,1024]{4,3,1,2,0:T(8,128)(2,1)}, u32[]{:S(2)}, u32[]{:S(2)}) %all-to-all-start.1) | async-done | bytes 8388640 | tf_op jit(solution)/shard_map/all_to_all | solution.py:89
  227.7 8.5 %copy.325 = bf16[16,8,2,16,1024]{4,3,1,0,2:T(8,128)(2,1)} copy(bf16[16,8,2,16,1024]{4,3,1,2,0:T(8,128)(2,1)} %all-to-all-done.1) | data formatting | bytes 16777216 | tf_op jit(solution)/shard_map/all_to_all | solution.py:89
  236.3 5.4 %fusion.255 = (bf16[128,1,16,1024]{3,2,0,1:T(8,128)(2,1)}, bf16[128,1,16,1024]{3,2,0,1:T(8,128)(2,1)S(1)}) fusion(bf16[128,2,16,1024]{3,2,0,1:T(8,128)(2,1)} %bitcast.734), kind=kLoop, calls=%fused_computation.416 | loop fusion | bytes 16777216 | tf_op jit(solution)/shard_map/slice | solution.py:113
  242.7 1.6 fusion.280
  244.3 1.6 fusion.279
  245.9 1.6 fusion.278
  247.5 1.6 fusion.277
  249.1 1.6 fusion.276
  250.7 1.6 fusion.275
  253.2 4.5 %fusion.273 = (f32[8,128]{1,0:T(8,128)}, f32[8,128,2048]{1,2,0:T(8,128)}) fusion(bf16[128,8,128]{0,2,1:T(8,128)(2,1)S(1)} %bitcast.778, bf16[2048,1024]{1,0:T(8,128)(2,1)S(1)} %bitcast.743, pred[2048]{0:T(1024)(128)(4,1)S(1)} %fusion.218), kind=kOutput, calls=%fused_computation.434 | convolution fusion | flops 543161344 | bytes 9181184 | tf_op jit(solution)/shard_map/rgd,ld->grl/dot_general | solution.py:26
  257.7 4.5 %fusion.271 = (f32[8,128]{1,0:T(8,128)}, f32[8,128,2048]{1,2,0:T(8,128)}) fusion(bf16[128,8,128]{0,2,1:T(8,128)(2,1)S(1)} %bitcast.782, bf16[2048,1024]{1,0:T(8,128)(2,1)S(1)} %bitcast.744, pred[2048]{0:T(1024)(128)(4,1)S(1)} %fusion.218), kind=kOutput, calls=%fused_computation.432 | convolution fusion | flops 543161344 | bytes 9181184 | tf_op jit(solution)/shard_map/rgd,ld->grl/dot_general | solution.py:26
  262.2 4.5 %fusion.269 = (f32[8,128]{1,0:T(8,128)}, f32[8,128,2048]{1,2,0:T(8,128)}) fusion(bf16[128,8,128]{0,2,1:T(8,128)(2,1)S(1)} %bitcast.780, bf16[2048,1024]{1,0:T(8,128)(2,1)S(1)} %bitcast.745, pred[2048]{0:T(1024)(128)(4,1)S(1)} %fusion.218), kind=kOutput, calls=%fused_computation.430 | convolution fusion | flops 543161344 | bytes 9181184 | tf_op jit(solution)/shard_map/rgd,ld->grl/dot_general | solution.py:26
  266.7 4.5 %fusion.267 = (f32[8,128]{1,0:T(8,128)}, f32[8,128,2048]{1,2,0:T(8,128)}) fusion(bf16[128,8,128]{0,2,1:T(8,128)(2,1)S(1)} %bitcast.776, bf16[2048,1024]{1,0:T(8,128)(2,1)S(1)} %bitcast.746, pred[2048]{0:T(1024)(128)(4,1)S(1)} %fusion.218), kind=kOutput, calls=%fused_computation.428 | convolution fusion | flops 543161344 | bytes 9181184 | tf_op jit(solution)/shard_map/rgd,ld->grl/dot_general | solution.py:26
  271.2 4.5 %fusion.265 = (f32[8,128]{1,0:T(8,128)}, f32[8,128,2048]{1,2,0:T(8,128)}) fusion(bf16[128,8,128]{0,2,1:T(8,128)(2,1)S(1)} %bitcast.774, bf16[2048,1024]{1,0:T(8,128)(2,1)S(1)} %bitcast.747, pred[2048]{0:T(1024)(128)(4,1)S(1)} %fusion.218), kind=kOutput, calls=%fused_computation.426 | convolution fusion | flops 543161344 | bytes 9181184 | tf_op jit(solution)/shard_map/rgd,ld->grl/dot_general | solution.py:26
  275.7 4.5 %fusion.263 = (f32[8,128]{1,0:T(8,128)}, f32[8,128,2048]{1,2,0:T(8,128)}) fusion(bf16[128,8,128]{0,2,1:T(8,128)(2,1)S(1)} %bitcast.772, bf16[2048,1024]{1,0:T(8,128)(2,1)S(1)} %bitcast.748, pred[2048]{0:T(1024)(128)(4,1)S(1)} %fusion.218), kind=kOutput, calls=%fused_computation.424 | convolution fusion | flops 543161344 | bytes 9181184 | tf_op jit(solution)/shard_map/rgd,ld->grl/dot_general | solution.py:26
  280.2 4.5 %fusion.261 = (f32[8,128]{1,0:T(8,128)}, f32[8,128,2048]{1,2,0:T(8,128)}) fusion(bf16[128,8,128]{0,2,1:T(8,128)(2,1)S(1)} %bitcast.770, bf16[2048,1024]{1,0:T(8,128)(2,1)S(1)} %bitcast.749, pred[2048]{0:T(1024)(128)(4,1)S(1)} %fusion.218), kind=kOutput, calls=%fused_computation.422 | convolution fusion | flops 543161344 | bytes 9181184 | tf_op jit(solution)/shard_map/rgd,ld->grl/dot_general | solution.py:26
  284.7 4.8 %fusion.259 = (f32[8,128]{1,0:T(8,128)}, f32[8,128,2048]{1,2,0:T(8,128)}) fusion(bf16[128,8,128]{0,2,1:T(8,128)(2,1)S(1)} %bitcast.768, bf16[2048,1024]{1,0:T(8,128)(2,1)S(1)} %bitcast.750, pred[2048]{0:T(1024)(128)(4,1)S(1)} %fusion.218), kind=kOutput, calls=%fused_computation.420 | convolution fusion | flops 543161344 | bytes 9181184 | tf_op jit(solution)/shard_map/rgd,ld->grl/dot_general | solution.py:26
  289.7 1.8 fusion.168
  298.8 1.5 fusion.172
  310.0 1.5 fusion.178
  321.2 4.2 %fusion.8 = (f32[8,128]{1,0:T(8,128)S(1)}, bf16[8,128,2176]{1,2,0:T(8,128)(2,1)S(1)}) fusion(f32[8,128,2048]{1,2,0:T(8,128)} %get-tuple-element.110, f32[8,128,128]{1,2,0:T(8,128)S(1)} %copy-done.5, f32[8,128]{1,0:T(8,128)S(1)} %reduce_max.295), kind=kLoop, calls=%fused_computation.26 | loop fusion | flops 8911872 | bytes 13377536 | tf_op jit(solution)/shard_map/reduce_sum | solution.py:37
  325.5 1.9 fusion.77
  327.8 4.2 %fusion.10 = (f32[8,128]{1,0:T(8,128)S(1)}, bf16[8,128,2176]{1,2,0:T(8,128)(2,1)S(1)}) fusion(f32[8,128,2048]{1,2,0:T(8,128)} %get-tuple-element.106, f32[8,128,128]{1,2,0:T(8,128)S(1)} %copy-done.4, f32[8,128]{1,0:T(8,128)S(1)} %reduce_max.292), kind=kLoop, calls=%fused_computation.28 | loop fusion | flops 8911872 | bytes 13377536 | tf_op jit(solution)/shard_map/reduce_sum | solution.py:37
  332.1 1.9 fusion.74
  334.4 4.2 %fusion.12 = (f32[8,128]{1,0:T(8,128)S(1)}, bf16[8,128,2176]{1,2,0:T(8,128)(2,1)S(1)}) fusion(f32[8,128,2048]{1,2,0:T(8,128)} %get-tuple-element.102, f32[8,128,128]{1,2,0:T(8,128)S(1)} %copy-done.3, f32[8,128]{1,0:T(8,128)S(1)} %reduce_max.289), kind=kLoop, calls=%fused_computation.30 | loop fusion | flops 8911872 | bytes 13377536 | tf_op jit(solution)/shard_map/reduce_sum | solution.py:37
  338.7 1.9 fusion.71
  341.0 4.2 %fusion.14 = (f32[8,128]{1,0:T(8,128)S(1)}, bf16[8,128,2176]{1,2,0:T(8,128)(2,1)S(1)}) fusion(f32[8,128,2048]{1,2,0:T(8,128)} %get-tuple-element.98, f32[8,128,128]{1,2,0:T(8,128)S(1)} %copy-done.2, f32[8,128]{1,0:T(8,128)S(1)} %reduce_max.286), kind=kLoop, calls=%fused_computation.32 | loop fusion | flops 8911872 | bytes 13377536 | tf_op jit(solution)/shard_map/reduce_sum | solution.py:37
  345.2 1.9 fusion.68
  347.5 4.2 %fusion.16 = (f32[8,128]{1,0:T(8,128)S(1)}, bf16[8,128,2176]{1,2,0:T(8,128)(2,1)S(1)}) fusion(f32[8,128,2048]{1,2,0:T(8,128)} %get-tuple-element.94, f32[8,128,128]{1,2,0:T(8,128)S(1)} %copy-done.1, f32[8,128]{1,0:T(8,128)S(1)} %reduce_max.283), kind=kLoop, calls=%fused_computation.34 | loop fusion | flops 8911872 | bytes 13377536 | tf_op jit(solution)/shard_map/reduce_sum | solution.py:37
  351.8 1.9 fusion.65
  354.7 4.3 %fusion.18 = (f32[8,128]{1,0:T(8,128)S(1)}, bf16[8,128,2176]{1,2,0:T(8,128)(2,1)S(1)}) fusion(f32[8,128,2048]{1,2,0:T(8,128)} %get-tuple-element.90, f32[8,128,128]{1,2,0:T(8,128)S(1)} %copy-done, f32[8,128]{1,0:T(8,128)S(1)} %reduce_max.280), kind=kLoop, calls=%fused_computation.36 | loop fusion | flops 8911872 | bytes 13377536 | tf_op jit(solution)/shard_map/reduce_sum | solution.py:37
  359.0 1.8 fusion.62
  361.2 4.2 %fusion.20 = (f32[8,128]{1,0:T(8,128)S(1)}, bf16[8,128,2176]{1,2,0:T(8,128)(2,1)S(1)}) fusion(f32[8,128,2048]{1,2,0:T(8,128)} %get-tuple-element.86, f32[8,128,128]{1,2,0:T(8,128)S(1)} %get-tuple-element.84, f32[8,128]{1,0:T(8,128)S(1)} %reduce_max.277), kind=kLoop, calls=%fused_computation.38 | loop fusion | flops 8911872 | bytes 13377536 | tf_op jit(solution)/shard_map/reduce_sum | solution.py:37
  365.5 1.8 fusion.59
  367.7 4.2 %fusion.22 = (f32[8,128]{1,0:T(8,128)S(1)}, bf16[8,128,2176]{1,2,0:T(8,128)(2,1)S(1)}) fusion(f32[8,128,2048]{1,2,0:T(8,128)} %get-tuple-element.82, f32[8,128,128]{1,2,0:T(8,128)S(1)} %get-tuple-element.80, f32[8,128]{1,0:T(8,128)S(1)} %reduce_max.274), kind=kLoop, calls=%fused_computation.40 | loop fusion | flops 8911872 | bytes 13377536 | tf_op jit(solution)/shard_map/reduce_sum | solution.py:37
  372.0 1.9 fusion.56
  (275 shorter events, 66.4 us)
Async XLA Ops:
  41.0 7.3 %copy-start.39 = (bf16[2,4,1024]{2,1,0:T(4,128)(2,1)S(1)}, bf16[2,4,1024]{2,1,0:T(4,128)(2,1)}, u32[]{:S(2)}) copy-start(bf16[2,4,1024]{2,1,0:T(4,128)(2,1)} %param.12) | copy-start | bytes 49156
  41.0 7.3 %copy-start.27 = (bf16[4,8192]{1,0:T(4,128)(2,1)S(1)}, bf16[4,8192]{1,0:T(4,128)(2,1)}, u32[]{:S(2)}) copy-start(bf16[4,8192]{1,0:T(4,128)(2,1)} %param.10) | copy-start | bytes 196612
  41.0 14.4 %copy-start.6 = (bf16[128,8192]{1,0:T(8,128)(2,1)S(1)}, bf16[128,8192]{1,0:T(8,128)(2,1)}, u32[]{:S(2)}) copy-start(bf16[128,8192]{1,0:T(8,128)(2,1)} %param.9) | copy-start | bytes 6291460
  41.0 186.8 %all-to-all-start.1 = ((bf16[16,8,2,16,1024]{4,3,1,2,0:T(8,128)(2,1)}), bf16[16,8,2,16,1024]{4,3,1,2,0:T(8,128)(2,1)}, u32[]{:S(2)}, u32[]{:S(2)}) async-start(bf16[16,8,2,16,1024]{4,3,1,2,0:T(8,128)(2,1)} %copy.324), calls=%async_computation.1 | async-start | bytes 16777216 | tf_op jit(solution)/shard_map/all_to_all | solution.py:89
  48.6 241.0 %copy-start.26 = (f32[4,1,8]{1,2,0:T(8,128)}, f32[4,1,8]{1,2,0:T(8,128)S(1)}, u32[]{:S(2)}) copy-start(f32[4,1,8]{1,2,0:T(8,128)S(1)} %copy.402) | copy-start | bytes 388
  62.6 8.5 %copy-start.7 = (bf16[128,1024]{1,0:T(8,128)(2,1)S(1)}, bf16[128,1024]{1,0:T(8,128)(2,1)}, u32[]{:S(2)}) copy-start(bf16[128,1024]{1,0:T(8,128)(2,1)} %get-tuple-element.31) | copy-start | bytes 786436
  62.6 13.8 %copy-start.61 = (s32[4]{0:T(128)S(1)}, s32[4]{0:T(128)}, u32[]{:S(2)}) copy-start(s32[4]{0:T(128)} %param.17) | copy-start | bytes 52
  284.7 9.6 %copy-start.14 = (f32[8,4,2048]{2,0,1:T(8,128)S(1)}, f32[8,4,2048]{2,0,1:T(8,128)}, u32[]{:S(2)}) copy-start(f32[8,4,2048]{2,0,1:T(8,128)} %get-tuple-element.124) | copy-start | bytes 786436
  284.7 14.0 %copy-start.13 = (f32[8,4,2048]{2,0,1:T(8,128)S(1)}, f32[8,4,2048]{2,0,1:T(8,128)}, u32[]{:S(2)}) copy-start(f32[8,4,2048]{2,0,1:T(8,128)} %get-tuple-element.122) | copy-start | bytes 786436
  284.7 17.8 %copy-start.12 = (f32[8,4,2048]{2,0,1:T(8,128)S(1)}, f32[8,4,2048]{2,0,1:T(8,128)}, u32[]{:S(2)}) copy-start(f32[8,4,2048]{2,0,1:T(8,128)} %get-tuple-element.120) | copy-start | bytes 786436
  284.7 21.6 %copy-start.11 = (f32[8,4,2048]{2,0,1:T(8,128)S(1)}, f32[8,4,2048]{2,0,1:T(8,128)}, u32[]{:S(2)}) copy-start(f32[8,4,2048]{2,0,1:T(8,128)} %get-tuple-element.118) | copy-start | bytes 786436
  284.7 25.3 %copy-start.10 = (f32[8,4,2048]{2,0,1:T(8,128)S(1)}, f32[8,4,2048]{2,0,1:T(8,128)}, u32[]{:S(2)}) copy-start(f32[8,4,2048]{2,0,1:T(8,128)} %get-tuple-element.116) | copy-start | bytes 786436
  284.7 29.1 %copy-start.9 = (f32[8,4,2048]{2,0,1:T(8,128)S(1)}, f32[8,4,2048]{2,0,1:T(8,128)}, u32[]{:S(2)}) copy-start(f32[8,4,2048]{2,0,1:T(8,128)} %get-tuple-element.114) | copy-start | bytes 786436
  289.5 31.7 %copy-start.5 = (f32[8,128,128]{1,2,0:T(8,128)S(1)}, f32[8,128,128]{1,2,0:T(8,128)}, u32[]{:S(2)}) copy-start(f32[8,128,128]{1,2,0:T(8,128)} %get-tuple-element.108) | copy-start | bytes 1572868
  300.3 25.2 %copy-start.17 = (bf16[8,4,2049]{2,0,1:T(8,128)(2,1)}, bf16[8,4,2049]{2,0,1:T(8,128)(2,1)S(1)}, u32[]{:S(2)}) copy-start(bf16[8,4,2049]{2,0,1:T(8,128)(2,1)S(1)} %get-tuple-element.37) | copy-start | bytes 393412
  304.0 21.4 %copy-start.19 = (bf16[8,4,2049]{2,0,1:T(8,128)(2,1)}, bf16[8,4,2049]{2,0,1:T(8,128)(2,1)S(1)}, u32[]{:S(2)}) copy-start(bf16[8,4,2049]{2,0,1:T(8,128)(2,1)S(1)} %get-tuple-element.39) | copy-start | bytes 393412
  307.8 17.7 %copy-start.21 = (bf16[8,4,2049]{2,0,1:T(8,128)(2,1)}, bf16[8,4,2049]{2,0,1:T(8,128)(2,1)S(1)}, u32[]{:S(2)}) copy-start(bf16[8,4,2049]{2,0,1:T(8,128)(2,1)S(1)} %get-tuple-element.41) | copy-start | bytes 393412
  311.6 13.9 %copy-start.23 = (bf16[8,4,2049]{2,0,1:T(8,128)(2,1)}, bf16[8,4,2049]{2,0,1:T(8,128)(2,1)S(1)}, u32[]{:S(2)}) copy-start(bf16[8,4,2049]{2,0,1:T(8,128)(2,1)S(1)} %get-tuple-element.43) | copy-start | bytes 393412
  315.3 10.2 %copy-start.25 = (bf16[8,4,2049]{2,0,1:T(8,128)(2,1)}, bf16[8,4,2049]{2,0,1:T(8,128)(2,1)S(1)}, u32[]{:S(2)}) copy-start(bf16[8,4,2049]{2,0,1:T(8,128)(2,1)S(1)} %get-tuple-element.45) | copy-start | bytes 393412
  325.5 2.3 copy-start.34
  325.5 2.3 copy-start.4
  351.8 2.9 copy-start
  371.9 2.5 copy-start.46
  371.9 2.5 copy-start.53
  371.9 2.5 copy-start.60
  371.9 4.5 %copy-start.24 = (bf16[8,4,2049]{2,0,1:T(8,128)(2,1)S(1)}, bf16[8,4,2049]{2,0,1:T(8,128)(2,1)}, u32[]{:S(2)}) copy-start(bf16[8,4,2049]{2,0,1:T(8,128)(2,1)} %copy-done.23) | copy-start | bytes 393412
  371.9 4.5 %copy-start.45 = (f32[8,4]{0,1:T(4,128)S(1)}, f32[8,4]{0,1:T(4,128)}, u32[]{:S(2)}) copy-start(f32[8,4]{0,1:T(4,128)} %get-tuple-element.42) | copy-start | bytes 388
  372.0 4.5 %copy-start.52 = (f32[4,128]{1,0:T(4,128)S(1)}, f32[4,128]{1,0:T(4,128)}, u32[]{:S(2)}) copy-start(f32[4,128]{1,0:T(4,128)} %get-tuple-element.63) | copy-start | bytes 6148
  372.0 4.5 %copy-start.59 = (f32[8,4]{0,1:T(4,128)S(1)}, f32[8,4]{0,1:T(4,128)}, u32[]{:S(2)}) copy-start(f32[8,4]{0,1:T(4,128)} %convert_reduce_fusion.5) | copy-start | bytes 388
  372.0 6.4 %copy-start.22 = (bf16[8,4,2049]{2,0,1:T(8,128)(2,1)S(1)}, bf16[8,4,2049]{2,0,1:T(8,128)(2,1)}, u32[]{:S(2)}) copy-start(bf16[8,4,2049]{2,0,1:T(8,128)(2,1)} %copy-done.21) | copy-start | bytes 393412
  372.0 6.4 %copy-start.44 = (f32[8,4]{0,1:T(4,128)S(1)}, f32[8,4]{0,1:T(4,128)}, u32[]{:S(2)}) copy-start(f32[8,4]{0,1:T(4,128)} %get-tuple-element.40) | copy-start | bytes 388
  372.0 6.4 %copy-start.51 = (f32[4,128]{1,0:T(4,128)S(1)}, f32[4,128]{1,0:T(4,128)}, u32[]{:S(2)}) copy-start(f32[4,128]{1,0:T(4,128)} %get-tuple-element.62) | copy-start | bytes 6148
  372.0 6.4 %copy-start.58 = (f32[8,4]{0,1:T(4,128)S(1)}, f32[8,4]{0,1:T(4,128)}, u32[]{:S(2)}) copy-start(f32[8,4]{0,1:T(4,128)} %convert_reduce_fusion.4) | copy-start | bytes 388
  373.9 6.4 %copy-start.20 = (bf16[8,4,2049]{2,0,1:T(8,128)(2,1)S(1)}, bf16[8,4,2049]{2,0,1:T(8,128)(2,1)}, u32[]{:S(2)}) copy-start(bf16[8,4,2049]{2,0,1:T(8,128)(2,1)} %copy-done.19) | copy-start | bytes 393412
  373.9 6.4 %copy-start.43 = (f32[8,4]{0,1:T(4,128)S(1)}, f32[8,4]{0,1:T(4,128)}, u32[]{:S(2)}) copy-start(f32[8,4]{0,1:T(4,128)} %get-tuple-element.38) | copy-start | bytes 388
  373.9 6.4 %copy-start.50 = (f32[4,128]{1,0:T(4,128)S(1)}, f32[4,128]{1,0:T(4,128)}, u32[]{:S(2)}) copy-start(f32[4,128]{1,0:T(4,128)} %get-tuple-element.61) | copy-start | bytes 6148
  373.9 6.4 %copy-start.57 = (f32[8,4]{0,1:T(4,128)S(1)}, f32[8,4]{0,1:T(4,128)}, u32[]{:S(2)}) copy-start(f32[8,4]{0,1:T(4,128)} %convert_reduce_fusion.3) | copy-start | bytes 388
  373.9 8.3 %copy-start.18 = (bf16[8,4,2049]{2,0,1:T(8,128)(2,1)S(1)}, bf16[8,4,2049]{2,0,1:T(8,128)(2,1)}, u32[]{:S(2)}) copy-start(bf16[8,4,2049]{2,0,1:T(8,128)(2,1)} %copy-done.17) | copy-start | bytes 393412
  373.9 8.3 %copy-start.42 = (f32[8,4]{0,1:T(4,128)S(1)}, f32[8,4]{0,1:T(4,128)}, u32[]{:S(2)}) copy-start(f32[8,4]{0,1:T(4,128)} %get-tuple-element.36) | copy-start | bytes 388
  374.0 8.2 %copy-start.49 = (f32[4,128]{1,0:T(4,128)S(1)}, f32[4,128]{1,0:T(4,128)}, u32[]{:S(2)}) copy-start(f32[4,128]{1,0:T(4,128)} %get-tuple-element.60) | copy-start | bytes 6148
  374.0 8.2 %copy-start.56 = (f32[8,4]{0,1:T(4,128)S(1)}, f32[8,4]{0,1:T(4,128)}, u32[]{:S(2)}) copy-start(f32[8,4]{0,1:T(4,128)} %convert_reduce_fusion.2) | copy-start | bytes 388
  374.0 10.1 %copy-start.16 = (bf16[8,4,2049]{2,0,1:T(8,128)(2,1)S(1)}, bf16[8,4,2049]{2,0,1:T(8,128)(2,1)}, u32[]{:S(2)}) copy-start(bf16[8,4,2049]{2,0,1:T(8,128)(2,1)} %copy-done.15) | copy-start | bytes 393412
  374.0 10.1 %copy-start.41 = (f32[8,4]{0,1:T(4,128)S(1)}, f32[8,4]{0,1:T(4,128)}, u32[]{:S(2)}) copy-start(f32[8,4]{0,1:T(4,128)} %get-tuple-element.34) | copy-start | bytes 388
  374.0 10.1 %copy-start.48 = (f32[4,128]{1,0:T(4,128)S(1)}, f32[4,128]{1,0:T(4,128)}, u32[]{:S(2)}) copy-start(f32[4,128]{1,0:T(4,128)} %get-tuple-element.59) | copy-start | bytes 6148
  374.0 10.1 %copy-start.55 = (f32[8,4]{0,1:T(4,128)S(1)}, f32[8,4]{0,1:T(4,128)}, u32[]{:S(2)}) copy-start(f32[8,4]{0,1:T(4,128)} %convert_reduce_fusion.1) | copy-start | bytes 388
  374.0 12.0 %copy-start.40 = (f32[8,4]{0,1:T(4,128)S(1)}, f32[8,4]{0,1:T(4,128)}, u32[]{:S(2)}) copy-start(f32[8,4]{0,1:T(4,128)} %get-tuple-element.32) | copy-start | bytes 388
  374.0 12.0 %copy-start.47 = (f32[4,128]{1,0:T(4,128)S(1)}, f32[4,128]{1,0:T(4,128)}, u32[]{:S(2)}) copy-start(f32[4,128]{1,0:T(4,128)} %get-tuple-element.58) | copy-start | bytes 6148
  374.0 12.0 %copy-start.54 = (f32[8,4]{0,1:T(4,128)S(1)}, f32[8,4]{0,1:T(4,128)}, u32[]{:S(2)}) copy-start(f32[8,4]{0,1:T(4,128)} %convert_reduce_fusion) | copy-start | bytes 388
  (15 other events, 31.1 us)
where the time goes:
time: 394 us; the launch traced here: 389 us
  waiting for transfers between devices  151 us (38%)
  matrix products  88 us (22%)
  other arithmetic  69.8 us (18%)
  local copies, waits for them, and re-layouts  60.2 us (15%)
  blocking collectives  11.1 us (3%)
  starting transfers between devices  6.58 us (2%)
    all_to_all x1, waiting for transfers between devices, on_device(): lax.all_to_all(served, 'pool', split_axis=0, concat_axis=0, tiled=True)  151 us
    dot_general x24, matrix products, attend(): jnp.einsum('rgd,ld->grl', head_queries, key_part, preferred_element_type=...  60.1 us
    reduce_sum x16, other arithmetic, attend(): totals = jnp.sum(terms, axis=2)  45.8 us
    dot_general x24, matrix products, attend(): jnp.einsum('grl,ld->rgd', weight_part, value_part, preferred_element_type...  26.9 us
    unnamed x148, local copies, waits for them, and re-layouts  11.7 us
    all_to_all x1, blocking collectives, on_device(): lax.all_to_all(requests, 'pool', split_axis=0, concat_axis=0, tiled=True)  11.1 us
    gather x1, local copies, waits for them, and re-layouts, on_device(): jnp.take(pool_pages, incoming.reshape(-1), axis=0)  8.61 us
    select_n x1, local copies, waits for them, and re-layouts, on_device(): jnp.take(pool_pages, incoming.reshape(-1), axis=0)  8.51 us
  transfers between devices with their start and end apart: 1, of which 1 were waited for; matrix products, arithmetic and copies ran while one was open for 7% of the time, Pallas kernels for 0%

commit v1 on v0

v1 whole, which is shorter than its diff:
```python
import functools
import math

import jax
import jax.numpy as jnp
from jax import lax
from jax.experimental import pallas as pl
from jax.experimental.pallas import tpu as pltpu
from jax.sharding import PartitionSpec as P

HEADS = 64
HEAD_DIM = 128
PRE_PAGES = 48
DEC_PAGES = 12
LOG2_SCALE = math.log2(math.e) / math.sqrt(HEAD_DIM)
CONTRACT_LAST = (((1,), (1,)), ((), ()))


def scores_of(queries, keys):
    return lax.dot_general(queries, keys, CONTRACT_LAST, preferred_element_type=jnp.float32)


def weigh(score_parts, value_parts):
    highest = functools.reduce(
        jnp.maximum, [jnp.max(s, axis=1, keepdims=True) for s in score_parts]
    )
    total = 0.0
    summed = 0.0
    for scores, values in zip(score_parts, value_parts):
        terms = jnp.exp2((scores - highest) * LOG2_SCALE)
        total = total + jnp.sum(terms, axis=1, keepdims=True)
        summed = summed + jnp.dot(
            terms.astype(jnp.bfloat16), values, preferred_element_type=jnp.float32
        )
    return summed / total


def attention_kernel(
    places, prefix_length, context_length,
    queries, decode_queries, entries, decode_entries, pages,
    output, decode_output, cache, sem,
):
    page_count, _, page_tokens, _ = cache.shape
    head = pl.program_id(0)
    row_count = queries.shape[0]
    group = queries.shape[1] // HEAD_DIM

    @pl.when(head == 0)
    def _():
        def fetch(t, carry):
            pltpu.make_async_copy(pages.at[places[t]], cache.at[t], sem).start()
            return carry

        lax.fori_loop(0, page_count, fetch, 0)
        pltpu.make_async_copy(cache, cache, sem).wait()

    columns = pl.ds(pl.multiple_of(head * HEAD_DIM, HEAD_DIM), HEAD_DIM)
    span = PRE_PAGES * page_tokens
    prefix_keys = cache[:PRE_PAGES, 0, :, columns].reshape(span, HEAD_DIM)
    prefix_values = cache[:PRE_PAGES, 1, :, columns].reshape(span, HEAD_DIM)
    position = lax.broadcasted_iota(jnp.int32, (1, span), 1)
    prefix_bias = jnp.where(position < prefix_length[0], 0.0, -jnp.inf)
    causal_bias = jnp.where(
        lax.broadcasted_iota(jnp.int32, (row_count, row_count), 0)
        >= lax.broadcasted_iota(jnp.int32, (row_count, row_count), 1),
        0.0,
        -jnp.inf,
    )
    own_keys = entries[0]
    own_values = entries[1]
    step = 4
    for start in range(0, group, step):
        stacked = jnp.concatenate(
            [queries[:, g * HEAD_DIM : (g + 1) * HEAD_DIM] for g in range(start, start + step)],
            axis=0,
        )
        own_scores = scores_of(stacked, own_keys).reshape(step, row_count, row_count)
        own_scores = (own_scores + causal_bias[None]).reshape(step * row_count, row_count)
        prefix_scores = scores_of(stacked, prefix_keys) + prefix_bias
        result = weigh([own_scores, prefix_scores], [own_values, prefix_values])
        result = result.astype(jnp.bfloat16)
        for g in range(step):
            output[:, (start + g) * HEAD_DIM : (start + g + 1) * HEAD_DIM] = result[
                g * row_count : (g + 1) * row_count
            ]

    context_span = (page_count - PRE_PAGES) * page_tokens
    row_span = DEC_PAGES * page_tokens
    context_keys = cache[PRE_PAGES:, 0, :, columns].reshape(context_span, HEAD_DIM)
    context_values = cache[PRE_PAGES:, 1, :, columns].reshape(context_span, HEAD_DIM)
    row_queries = decode_queries[0]
    shape = (row_queries.shape[0], context_span)
    row = lax.broadcasted_iota(jnp.int32, shape, 0) // group
    place = lax.broadcasted_iota(jnp.int32, shape, 1)
    usable = jnp.zeros(shape, jnp.bool_)
    for r in range(context_span // row_span):
        usable = usable | (
            (row == r) & (place >= r * row_span) & (place < r * row_span + context_length[r])
        )
    context_scores = jnp.where(usable, scores_of(row_queries, context_keys), -jnp.inf)
    new_scores = scores_of(row_queries, decode_entries[0])
    own = lax.broadcasted_iota(jnp.int32, new_scores.shape, 0) // group
    own = own == lax.broadcasted_iota(jnp.int32, new_scores.shape, 1)
    new_scores = jnp.where(own, new_scores, -jnp.inf)
    decode_output[0] = weigh(
        [new_scores, context_scores], [decode_entries[1], context_values]
    ).astype(jnp.bfloat16)


def attention(places, prefix_length, context_length, queries, decode_queries, entries,
              decode_entries, pages):
    row_count = queries.shape[0]
    decode_count = decode_queries.shape[0]
    key_heads = pages.shape[-1] // HEAD_DIM
    group = HEADS // key_heads
    page_count = places.shape[0]
    arranged = decode_queries.reshape(decode_count, key_heads, group, HEAD_DIM)
    arranged = jnp.transpose(arranged, (1, 0, 2, 3)).reshape(key_heads, -1, HEAD_DIM)
    padded = jnp.pad(decode_entries, ((0, 0), (0, -decode_count % 16), (0, 0)))
    output, decoded = pl.pallas_call(
        attention_kernel,
        grid_spec=pltpu.PrefetchScalarGridSpec(
            num_scalar_prefetch=3,
            grid=(key_heads,),
            in_specs=[
                pl.BlockSpec((row_count, group * HEAD_DIM), lambda h, *_: (0, h)),
                pl.BlockSpec((1,) + arranged.shape[1:], lambda h, *_: (h, 0, 0)),
                pl.BlockSpec((2, row_count, HEAD_DIM), lambda h, *_: (0, 0, h)),
                pl.BlockSpec((2, padded.shape[1], HEAD_DIM), lambda h, *_: (0, 0, h)),
                pl.BlockSpec(memory_space=pl.ANY),
            ],
            out_specs=[
                pl.BlockSpec((row_count, group * HEAD_DIM), lambda h, *_: (0, h)),
                pl.BlockSpec((1,) + arranged.shape[1:], lambda h, *_: (h, 0, 0)),
            ],
            scratch_shapes=[
                pltpu.VMEM((page_count,) + pages.shape[1:], pages.dtype),
                pltpu.SemaphoreType.DMA,
            ],
        ),
        out_shape=[
            jax.ShapeDtypeStruct(queries.shape, jnp.bfloat16),
            jax.ShapeDtypeStruct(arranged.shape, jnp.bfloat16),
        ],
        compiler_params=pltpu.CompilerParams(
            dimension_semantics=("arbitrary",), vmem_limit_bytes=40 * 1024 * 1024
        ),
        name="paged_attention",
    )(places, prefix_length, context_length, queries, arranged, entries, padded, pages)
    decoded = decoded.reshape(key_heads, decode_count, group, HEAD_DIM)
    decoded = jnp.transpose(decoded, (1, 0, 2, 3)).reshape(decode_queries.shape)
    return output, decoded


def on_device(
    stretch_queries,
    decode_queries,
    stretch_entries,
    decode_entries,
    pool_pages,
    page_owner,
    page_slot,
    prefix_length,
    context_length,
):
    pool_size = lax.axis_size("pool")
    page_count = page_slot.shape[0]
    capacity = max(2, 4 * page_count // (3 * pool_size))
    slot_total = pool_size * capacity
    owners = page_owner[:, 0]
    member = (owners[:, None] == jnp.arange(pool_size, dtype=jnp.int32)[None, :]).astype(jnp.int32)
    ranks = jnp.sum(jnp.cumsum(member, axis=0) * member, axis=1) - 1
    target = owners * capacity + ranks
    placed = target[:, None] == jnp.arange(slot_total, dtype=jnp.int32)[None, :]
    requests = jnp.sum(jnp.where(placed, page_slot[:, None], 0), axis=0).reshape(
        pool_size, capacity
    )
    incoming = lax.all_to_all(requests, "pool", split_axis=0, concat_axis=0, tiled=True)
    served = jnp.take(pool_pages, incoming.reshape(-1), axis=0).reshape(
        (pool_size, capacity) + pool_pages.shape[1:]
    )
    received = lax.all_to_all(served, "pool", split_axis=0, concat_axis=0, tiled=True)
    received = received.reshape((slot_total,) + pool_pages.shape[1:])
    return attention(
        target, prefix_length, context_length, stretch_queries, decode_queries,
        stretch_entries, decode_entries, received,
    )


def solution(mesh):
    rows = P(("replica", "pool"), None)
    entries = P(None, ("replica", "pool"), None)
    vector = P(("replica", "pool"))
    pages = P(("replica", "pool"), None, None, None)
    return jax.shard_map(
        on_device,
        mesh=mesh,
        in_specs=(rows, rows, entries, entries, pages, rows, vector, vector, vector),
        out_specs=(rows, rows),
        check_vma=False,
    )
```

time: 394 us -> 242 us (0.61)
  matrix products: 88 us -> 0 us
  other arithmetic: 69.8 us -> 11.2 us
  local copies, waits for them, and re-layouts: 60.2 us -> 10.3 us
  waiting for transfers between devices: 151 us -> 179 us
  Pallas kernels: 0 us -> 19 us
    dot_general x56 -> x0, matrix products: 88 us -> none  [the longest x24 60.1 us: attend(): jnp.einsum('rgd,ld->grl', head_queries, key_part, preferred_element_type=...]
    reduce_sum x16 -> x0, other arithmetic: 45.8 us -> none  [attend(): totals = jnp.sum(terms, axis=2)]
    all_to_all x1, waiting for transfers between devices: 151 us -> 179 us  [on_device(): lax.all_to_all(served, 'pool', split_axis=0, concat_axis=0, tiled=True)]
    pallas_call x0 -> x1, Pallas kernels: none -> 19 us  [attention(): pl.pallas_call(attention_kernel, grid_spec=pltpu.PrefetchScalarGridSpec(n...]
    unnamed x148 -> x14, local copies, waits for them, and re-layouts: 11.7 us -> 0.72 us
    all_to_all x1 -> x0, local copies, waits for them, and re-layouts: 8.51 us -> none  [on_device(): lax.all_to_all(served, 'pool', split_axis=0, concat_axis=0, tiled=True)]
    select_n x1 -> x0, local copies, waits for them, and re-layouts: 8.51 us -> none  [on_device(): jnp.take(pool_pages, incoming.reshape(-1), axis=0)]
    slice x3 -> x0, local copies, waits for them, and re-layouts: 8.22 us -> none  [the longest x1 5.45 us: on_device(): prefix_values = received[:, 1].reshape(slot_total * page_tokens, key_width)]
  transfers between devices with their start and end apart: 1 -> 1, of which waited for: 1 -> 1; matrix products, arithmetic and copies ran while one was open for 7% -> 0% of each run, Pallas kernels for 0% -> 0%
where the time goes in v1:
time: 242 us; the launch traced here: 239 us
  waiting for transfers between devices  179 us (74%)
  Pallas kernels  19 us (8%)
  other arithmetic  11.2 us (5%)
  blocking collectives  11.1 us (5%)
  local copies, waits for them, and re-layouts  10.3 us (4%)
  starting transfers between devices  6.54 us (3%)
    all_to_all x1, waiting for transfers between devices, on_device(): lax.all_to_all(served, 'pool', split_axis=0, concat_axis=0, tiled=True)  179 us
    pallas_call x1, Pallas kernels, attention(): pl.pallas_call(attention_kernel, grid_spec=pltpu.PrefetchScalarGridSpec(n...  19 us
    all_to_all x1, blocking collectives, on_device(): lax.all_to_all(requests, 'pool', split_axis=0, concat_axis=0, tiled=True)  11.1 us
    gather x1, local copies, waits for them, and re-layouts, on_device(): jnp.take(pool_pages, incoming.reshape(-1), axis=0)  8.68 us
    select_n x2, other arithmetic, on_device(): jnp.take(pool_pages, incoming.reshape(-1), axis=0)  7.42 us
    all_to_all x1, starting transfers between devices, on_device(): lax.all_to_all(served, 'pool', split_axis=0, concat_axis=0, tiled=True)  6.54 us
  transfers between devices with their start and end apart: 1, of which 1 were waited for; matrix products, arithmetic and copies ran while one was open for 0% of the time, Pallas kernels for 0%

profile of v1, /device:TPU:9, one launch (start us, length us, event | category | flops | bytes accessed | tf_op | source)
XLA Modules:
  0.0 239.0 jit_solution(17186061221471256692)
XLA Ops:
  0.6 0.7 fusion
  1.4 0.1 reduce_window_sum.11
  1.5 0.8 select_reduce_fusion.1
  2.3 0.7 fusion.2
  3.0 0.8 select_reduce_fusion
  3.8 0.1 all_to_all.9
  3.9 11.1 %all_to_all.14 = s32[16,1,8]{2,1,0:T(1,128)S(1)} all-to-all(s32[16,1,8]{2,1,0:T(1,128)S(1)} %bitcast.40), channel_id=1, replica_groups=mesh['replica'=2,'pool'=16] {'pool'}, dimensions={0} | all-to-all | bytes 1024 | tf_op jit(solution)/shard_map/all_to_all | solution.py:178
  15.0 0.5 broadcast.61
  15.5 0.7 reduce.3
  16.1 0.1 reshape.81
  16.3 0.1 copy.26
  16.3 0.1 copy.27
  16.4 8.7 %gather_fusion = bf16[128,2,16,1024]{3,2,1,0:T(8,128)(2,1)} fusion(bf16[64,2,16,1024]{3,2,1,0:T(8,128)(2,1)} %param.13, s32[1024]{0:T(1024)S(1)} %pad_clamp_fusion), kind=kCustom, calls=%fused_computation | custom fusion | bytes 16777728 | tf_op jit(solution)/shard_map/jit(_take)/gather | solution.py:179
  25.1 7.4 %broadcast_select_fusion = bf16[16,8,2,16,1024]{4,3,2,1,0:T(8,128)(2,1)} fusion(bf16[16,8,2,16,1024]{4,3,2,1,0:T(8,128)(2,1)} %bitcast.37, pred[16,8]{1,0:T(8,128)(4,1)S(1)} %copy.27), kind=kLoop, calls=%fused_computation.1 | loop fusion | flops 4194304 | bytes 16777344 | tf_op jit(solution)/shard_map/jit(_take)/select_n | solution.py:179
  32.5 0.0 copy-start.4
  32.5 0.0 copy-start.5
  32.5 0.0 copy-start.3
  32.5 0.0 copy-start
  32.5 0.0 copy-start.1
  32.5 0.0 copy-start.2
  32.6 6.5 %all-to-all-start.1 = ((bf16[16,8,2,16,1024]{4,3,2,1,0:T(8,128)(2,1)}), bf16[16,8,2,16,1024]{4,3,2,1,0:T(8,128)(2,1)}, u32[]{:S(2)}, u32[]{:S(2)}) async-start(bf16[16,8,2,16,1024]{4,3,2,1,0:T(8,128)(2,1)} %broadcast_select_fusion), calls=%async_computation.1 | async-start | bytes 16777216 | tf_op jit(solution)/shard_map/all_to_all | solution.py:182
  39.8 0.0 copy-done.4
  39.8 0.0 copy-done.5
  39.8 0.0 copy-done.3
  39.8 179.5 %all-to-all-done.1 = bf16[16,8,2,16,1024]{4,3,2,1,0:T(8,128)(2,1)} async-done(((bf16[16,8,2,16,1024]{4,3,2,1,0:T(8,128)(2,1)}), bf16[16,8,2,16,1024]{4,3,2,1,0:T(8,128)(2,1)}, u32[]{:S(2)}, u32[]{:S(2)}) %all-to-all-start.1) | async-done | bytes 8388640 | tf_op jit(solution)/shard_map/all_to_all | solution.py:182
  219.3 0.0 copy-done
  219.3 0.0 copy-done.1
  219.3 0.0 copy-done.2
  219.3 19.0 %paged_attention.1 = (bf16[128,8192]{1,0:T(8,128)(2,1)}, bf16[8,32,128]{2,1,0:T(8,128)(2,1)S(1)}) custom-call(s32[96]{0:T(128)S(1)} %multiply_add_fusion.places, s32[1]{0:T(128)S(6)} %copy.37.prefix_length, s32[4]{0:T(128)S(1)} %copy-done.2, bf16[128,8192]{1,0:T(8,128)(2,1)S(1)} %copy-done, bf16[8,32,128]{2,1,0:T(8,128)(2,1)S(1)} %copy_bitcast_fusion.3.decode_queries, ...), custom_call_target="tpu_custom_call" | custom-call | tf_op jit(solution)/shard_map/paged_attention/pallas_call | solution.py:120
  238.3 0.7 copy.36
  (7 shorter events, 0.1 us)
Async XLA Ops:
  32.5 7.2 %copy-start.4 = (bf16[2,4,1024]{2,1,0:T(4,128)(2,1)S(1)}, bf16[2,4,1024]{2,1,0:T(4,128)(2,1)}, u32[]{:S(2)}) copy-start(bf16[2,4,1024]{2,1,0:T(4,128)(2,1)} %param.12) | copy-start | bytes 49156
  32.5 7.3 %copy-start.5 = (s32[96,1]{0,1:T(1,128)S(1)}, s32[96,1]{0,1:T(1,128)}, u32[]{:S(2)}) copy-start(s32[96,1]{0,1:T(1,128)} %param.14) | copy-start | bytes 1156
  32.5 7.3 %copy-start.3 = (bf16[4,8192]{1,0:T(4,128)(2,1)S(1)}, bf16[4,8192]{1,0:T(4,128)(2,1)}, u32[]{:S(2)}) copy-start(bf16[4,8192]{1,0:T(4,128)(2,1)} %param.10) | copy-start | bytes 196612
  32.5 186.8 %copy-start = (bf16[128,8192]{1,0:T(8,128)(2,1)S(1)}, bf16[128,8192]{1,0:T(8,128)(2,1)}, u32[]{:S(2)}) copy-start(bf16[128,8192]{1,0:T(8,128)(2,1)} %queries.1) | copy-start | bytes 6291460
  32.5 186.8 %copy-start.1 = (bf16[2,128,1024]{2,1,0:T(8,128)(2,1)S(1)}, bf16[2,128,1024]{2,1,0:T(8,128)(2,1)}, u32[]{:S(2)}) copy-start(bf16[2,128,1024]{2,1,0:T(8,128)(2,1)} %entries.1) | copy-start | bytes 1572868
  32.5 186.8 %copy-start.2 = (s32[4]{0:T(128)S(1)}, s32[4]{0:T(128)}, u32[]{:S(2)}) copy-start(s32[4]{0:T(128)} %context_length.1) | copy-start | bytes 52
  32.6 186.7 %all-to-all-start.1 = ((bf16[16,8,2,16,1024]{4,3,2,1,0:T(8,128)(2,1)}), bf16[16,8,2,16,1024]{4,3,2,1,0:T(8,128)(2,1)}, u32[]{:S(2)}, u32[]{:S(2)}) async-start(bf16[16,8,2,16,1024]{4,3,2,1,0:T(8,128)(2,1)} %broadcast_select_fusion), calls=%async_computation.1 | async-start | bytes 16777216 | tf_op jit(solution)/shard_map/all_to_all | solution.py:182
